TPU v7x, 128 devices: a whole 4x4x4 slice. The times are simulated.
128 devices in a mesh: gx: 2 (over x_hi), gy: 4 (over y), gz: 16 (over x_lo, z, core).
Axes of the slice: x: 4 (x_hi: 2, x_lo: 2; x = x_hi * 2 + x_lo), y: 4, z: 4, core: 2. Of those that a mesh axis runs over, the one named last changes fastest.
Arguments:
- state_real: float32 [16777216], P(('gx', 'gy', 'gz'))
- state_imag: float32 [16777216], P(('gx', 'gy', 'gz'))
- adjoint_real: float32 [16777216], P(('gx', 'gy', 'gz'))
- adjoint_imag: float32 [16777216], P(('gx', 'gy', 'gz'))
- energies: int32 [16777216], P(('gx', 'gy', 'gz')), may hold values from 12 to 4324, as said below
- gamma_angle: float32 [1], replicated, may hold values from 0.02 to 0.1
- beta_angle: float32 [1], replicated, may hold values from 0.1 to 0.7
Outputs:
- input_real: float32 [16777216], P(('gx', 'gy', 'gz'))
- input_imag: float32 [16777216], P(('gx', 'gy', 'gz'))
- adjoint_in_real: float32 [16777216], P(('gx', 'gy', 'gz'))
- adjoint_in_imag: float32 [16777216], P(('gx', 'gy', 'gz'))
- gamma_gradient: float32 [1], replicated
- beta_gradient: float32 [1], replicated
Inputs may be any that keep to these rules, and one draw needn't show every extreme that they name: `energies`: entry j is the LABS energy sum over k from 1 to 23 of (sum over i of s_i s_(i+k))^2, with spins s_i = 1 - 2 b_i from the bits b of j XOR a mask of 24 bits drawn once.
All inputs are finite; a program needn't handle non-finite values.
Results may differ from a plain program's by a relative error of at most 0.00013.
Values sent between devices are 32-bit elements; how exact they have to be, the bound alone decides.
A program may use at most 64 MiB of HBM per device.

v0:
```python
import jax
import jax.numpy as jnp
from jax import lax
from jax.sharding import PartitionSpec as P


def count_ones(values, width):
    total = jnp.zeros_like(values)
    for bit_pos in range(width):
        total = total + (values >> bit_pos & 1)
    return total


def hadamard(group_bits):
    indices = jnp.arange(2**group_bits, dtype=jnp.int32)
    parity = count_ones(indices[:, None] & indices[None, :], group_bits) & 1
    return (1 - 2 * parity).astype(jnp.float32) * jnp.float32(2.0 ** (-0.5 * group_bits))


def walsh_local(values, total_bits):
    finished = 0
    while finished < total_bits:
        group_bits = min(7, total_bits - finished)
        lower_size = 2**finished
        upper_size = values.shape[1] // (lower_size * 2**group_bits)
        matrix = hadamard(group_bits)
        if finished == 0:
            shaped = values.reshape(values.shape[0], upper_size, 2**group_bits)
            shaped = jnp.einsum(
                "pak,km->pam",
                shaped,
                matrix,
                precision=lax.Precision.HIGHEST,
                preferred_element_type=jnp.float32,
            )
        else:
            shaped = values.reshape(values.shape[0], upper_size, 2**group_bits, lower_size)
            shaped = jnp.einsum(
                "pakl,km->paml",
                shaped,
                matrix,
                precision=lax.Precision.HIGHEST,
                preferred_element_type=jnp.float32,
            )
        values = shaped.reshape(values.shape[0], -1)
        finished += group_bits
    return values


def rotate_pair(real_part, imag_part, cosine_part, sine_part):
    return (
        real_part * cosine_part - imag_part * sine_part,
        real_part * sine_part + imag_part * cosine_part,
    )


def per_device(
    state_real, state_imag, adjoint_real, adjoint_imag, energies, gamma_angle, beta_angle
):
    local_size = state_real.shape[0]
    local_bits = local_size.bit_length() - 1
    devices = lax.axis_size(("gx", "gy", "gz"))
    global_bits = devices.bit_length() - 1
    row_size = local_size // devices
    row_bits = row_size.bit_length() - 1
    whole_size = local_size * devices
    stacked = jnp.stack([state_real, state_imag, adjoint_real, adjoint_imag])
    transformed = walsh_local(stacked, local_bits)
    exchanged = lax.all_to_all(
        transformed.reshape(4, devices, row_size),
        ("gx", "gy", "gz"),
        split_axis=1,
        concat_axis=1,
        tiled=True,
    )
    outer_matrix = hadamard(global_bits)
    spun_state = jnp.einsum(
        "pnr,nm->pmr",
        exchanged,
        outer_matrix,
        precision=lax.Precision.HIGHEST,
        preferred_element_type=jnp.float32,
    )
    source_ones = count_ones(jnp.arange(devices, dtype=jnp.int32), global_bits)
    row_ones = count_ones(jnp.arange(row_size, dtype=jnp.int32), row_bits)
    device_ones = count_ones(lax.axis_index(("gx", "gy", "gz")), global_bits)
    ones_total = source_ones[:, None] + row_ones[None, :] + device_ones
    eigenvalue = (local_bits + global_bits - 2 * ones_total).astype(jnp.float32)
    beta_part = jnp.sum(
        eigenvalue * (spun_state[2] * spun_state[1] - spun_state[3] * spun_state[0])
    )
    beta_total = lax.psum(beta_part, ("gx", "gy", "gz"))
    angle_beta = beta_angle[0] * eigenvalue
    cosine_part = jnp.cos(angle_beta)
    sine_part = jnp.sin(angle_beta)
    first_re, first_im = rotate_pair(spun_state[0], spun_state[1], cosine_part, sine_part)
    second_re, second_im = rotate_pair(spun_state[2], spun_state[3], cosine_part, sine_part)
    rotated = jnp.stack([first_re, first_im, second_re, second_im])
    unspun = jnp.einsum(
        "pnr,nm->pmr",
        rotated,
        outer_matrix,
        precision=lax.Precision.HIGHEST,
        preferred_element_type=jnp.float32,
    )
    returned = lax.all_to_all(unspun, ("gx", "gy", "gz"), split_axis=1, concat_axis=1, tiled=True)
    middle = walsh_local(returned.reshape(4, local_size), local_bits)
    energy_float = energies.astype(jnp.float32)
    gamma_part = jnp.sum(energy_float * (middle[2] * middle[1] - middle[3] * middle[0]))
    gamma_total = lax.psum(gamma_part, ("gx", "gy", "gz"))
    angle_gamma = gamma_angle[0] * energy_float
    cosine_cost = jnp.cos(angle_gamma)
    sine_cost = jnp.sin(angle_gamma)
    input_real, input_imag = rotate_pair(middle[0], middle[1], cosine_cost, sine_cost)
    adjoint_in_real, adjoint_in_imag = rotate_pair(middle[2], middle[3], cosine_cost, sine_cost)
    gamma_gradient = (gamma_total / whole_size).reshape(1)
    beta_gradient = (beta_total / whole_size).reshape(1)
    return (input_real, input_imag, adjoint_in_real, adjoint_in_imag, gamma_gradient, beta_gradient)


def solution(mesh):
    in_specs = (
        P(("gx", "gy", "gz")),
        P(("gx", "gy", "gz")),
        P(("gx", "gy", "gz")),
        P(("gx", "gy", "gz")),
        P(("gx", "gy", "gz")),
        P(),
        P(),
    )
    out_specs = (
        P(("gx", "gy", "gz")),
        P(("gx", "gy", "gz")),
        P(("gx", "gy", "gz")),
        P(("gx", "gy", "gz")),
        P(),
        P(),
    )
    return jax.shard_map(
        per_device, mesh=mesh, in_specs=in_specs, out_specs=out_specs, check_vma=False
    )
```

profile of v0, /device:TPU:1, one launch (start us, length us, event | category | flops | bytes accessed | tf_op | source)
XLA Modules:
  0.0 191.9 jit_solution(18394003207503415719)
XLA Ops:
  0.6 3.4 %fusion = f32[4,8,128,128]{3,2,1,0:T(8,128)S(1)} fusion(f32[1,8,128,128]{3,2,1,0:T(8,128)} %bitcast.86, f32[1,8,128,128]{3,2,1,0:T(8,128)} %bitcast.87, f32[1,8,128,128]{3,2,1,0:T(8,128)} %bitcast.88, f32[1,8,128,128]{3,2,1,0:T(8,128)} %bitcast.89), kind=kOutput, calls=%fused_computation.2 | convolution fusion | flops 807305216 | bytes 4194304 | tf_op jit(solution)/shard_map/pak,km->pam/dot_general | solution.py:29
  4.1 2.0 %convolution_bitcast_fusion.3 = f32[4,8,128,128]{3,2,1,0:T(8,128)S(1)} fusion(f32[4,8,128,128]{3,2,1,0:T(8,128)S(1)} %fusion), kind=kOutput, calls=%fused_computation.23 | convolution fusion | flops 805732352 | bytes 4194304 | tf_op jit(solution)/shard_map/pakl,km->paml/dot_general | solution.py:38
  6.0 1.6 reshape.260
  7.6 3.4 %convolution_bitcast_fusion.1 = f32[4,1,8,16384]{3,2,0,1:T(8,128)S(1)} fusion(f32[4,8,16384]{2,1,0:T(8,128)} %reshape.260), kind=kOutput, calls=%fused_computation.1 | convolution fusion | flops 50332544 | bytes 4194304 | tf_op jit(solution)/shard_map/pakl,km->paml/dot_general | solution.py:38
  11.0 1.5 reshape_reshape.2
  12.5 4.3 %copy.17 = f32[4,128,1024]{2,0,1:T(4,128)} copy(f32[4,128,1024]{2,1,0:T(8,128)} %reshape_reshape.2) | data formatting | bytes 4194304 | tf_op jit(solution)/shard_map/reshape;reshape | solution.py:70
  16.8 12.0 %all-to-all-start = ((f32[4,128,1024]{2,0,1:T(4,128)}), f32[4,128,1024]{2,0,1:T(4,128)}, u32[]{:S(2)}, u32[]{:S(2)}) async-start(f32[4,128,1024]{2,0,1:T(4,128)} %copy.17), calls=%async_computation | async-start | bytes 4194304 | tf_op jit(solution)/shard_map/all_to_all | solution.py:69
  29.5 29.4 %all-to-all-done = f32[4,128,1024]{2,0,1:T(4,128)} async-done(((f32[4,128,1024]{2,0,1:T(4,128)}), f32[4,128,1024]{2,0,1:T(4,128)}, u32[]{:S(2)}, u32[]{:S(2)}) %all-to-all-start) | async-done | bytes 2097184 | tf_op jit(solution)/shard_map/all_to_all | solution.py:69
  58.9 4.6 %fusion.18 = f32[4,128,1024]{2,1,0:T(8,128)S(1)} fusion(f32[4,128,1024]{2,0,1:T(4,128)} %all-to-all-done), kind=kOutput, calls=%fused_computation.20 | convolution fusion | flops 805732352 | bytes 4194304 | tf_op jit(solution)/shard_map/pnr,nm->pmr/dot_general | solution.py:77
  63.4 2.5 %multiply_subtract_fusion.3 = (f32[1,128,1024]{2,1,0:T(8,128)S(1)}, f32[1,128,1024]{2,1,0:T(8,128)S(1)}, f32[1,128,1024]{2,1,0:T(8,128)S(1)}, f32[1,128,1024]{2,1,0:T(8,128)S(1)}) fusion(f32[4,128,1024]{2,1,0:T(8,128)S(1)} %fusion.18, s32[]{:T(128)S(6)} %add.379, s32[1024]{0:T(1024)S(1)} %fusion.45, s32[128]{0:T(128)S(1)} %fusion.74, f32[]{:T(128)} %bitcast.81), kind=kLoop, calls=%fused_computation.39 | loop fusion | flops 2359296 | bytes 4198920 | tf_op jit(solution)/shard_map/sub | solution.py:52
  65.9 2.0 %fusion.21 = f32[4,128,1024]{2,1,0:T(8,128)S(1)} fusion(f32[1,128,1024]{2,1,0:T(8,128)S(1)} %get-tuple-element.10, f32[1,128,1024]{2,1,0:T(8,128)S(1)} %get-tuple-element.9, f32[1,128,1024]{2,1,0:T(8,128)S(1)} %get-tuple-element.11, f32[1,128,1024]{2,1,0:T(8,128)S(1)} %get-tuple-element.8), kind=kOutput, calls=%fused_computation.21 | convolution fusion | flops 807305216 | bytes 4194304 | tf_op jit(solution)/shard_map/pnr,nm->pmr/dot_general | solution.py:99
  67.9 2.7 %copy.19 = f32[4,128,1024]{2,0,1:T(4,128)} copy(f32[4,128,1024]{2,1,0:T(8,128)S(1)} %fusion.21) | data formatting | bytes 4194304 | tf_op jit(solution)/shard_map/pnr,nm->pmr/transpose | solution.py:99
  70.6 5.3 %all-to-all-start.1 = ((f32[4,128,1024]{2,0,1:T(4,128)}), f32[4,128,1024]{2,0,1:T(4,128)}, u32[]{:S(2)}, u32[]{:S(2)}) async-start(f32[4,128,1024]{2,0,1:T(4,128)} %copy.19), calls=%async_computation.1 | async-start | bytes 4194304 | tf_op jit(solution)/shard_map/all_to_all | solution.py:106
  76.5 1.0 fusion.24
  77.5 28.6 %all-to-all-done.1 = f32[4,128,1024]{2,0,1:T(4,128)} async-done(((f32[4,128,1024]{2,0,1:T(4,128)}), f32[4,128,1024]{2,0,1:T(4,128)}, u32[]{:S(2)}, u32[]{:S(2)}) %all-to-all-start.1) | async-done | bytes 2097184 | tf_op jit(solution)/shard_map/all_to_all | solution.py:106
  106.1 2.8 %copy.20 = f32[4,128,1024]{2,1,0:T(8,128)S(1)} copy(f32[4,128,1024]{2,0,1:T(4,128)} %all-to-all-done.1) | data formatting | bytes 4194304 | tf_op jit(solution)/shard_map/all_to_all | solution.py:106
  108.9 1.5 dot_general.36
  110.4 3.5 %fusion.29 = f32[4,8,128,128]{3,2,1,0:T(8,128)S(1)} fusion(f32[4,8,128,128]{3,2,1,0:T(8,128)} %dot_general.36), kind=kOutput, calls=%fused_computation.45 | convolution fusion | flops 805732352 | bytes 4194304 | tf_op jit(solution)/shard_map/pak,km->pam/dot_general | solution.py:29
  113.9 2.0 %convolution_bitcast_fusion.2 = f32[4,8,128,128]{3,2,1,0:T(8,128)S(1)} fusion(f32[4,8,128,128]{3,2,1,0:T(8,128)S(1)} %fusion.29), kind=kOutput, calls=%fused_computation.22 | convolution fusion | flops 805732352 | bytes 4194304 | tf_op jit(solution)/shard_map/pakl,km->paml/dot_general | solution.py:38
  115.9 1.6 reshape.261
  117.4 3.4 %convolution_bitcast_fusion = f32[4,1,8,16384]{3,2,0,1:T(8,128)S(1)} fusion(f32[4,8,16384]{2,1,0:T(8,128)} %reshape.261), kind=kOutput, calls=%fused_computation | convolution fusion | flops 50332544 | bytes 4194304 | tf_op jit(solution)/shard_map/pakl,km->paml/dot_general | solution.py:38
  120.8 0.1 slice_bitcast_fusion.1
  121.0 0.0 copy-start
  121.0 0.1 copy.29
  121.1 0.1 copy.30
  121.2 0.1 copy.28
  121.3 0.1 copy.27
  121.4 0.6 copy-done
  122.0 3.7 %multiply_reduce_fusion = (f32[]{:T(128)}, f32[131072]{0:T(1024)}, f32[131072]{0:T(1024)}, f32[131072]{0:T(1024)}, f32[131072]{0:T(1024)}) fusion(f32[131072]{0:T(1024)S(1)} %bitcast.83, f32[131072]{0:T(1024)S(1)} %bitcast.85, f32[131072]{0:T(1024)S(1)} %bitcast.82, f32[131072]{0:T(1024)S(1)} %bitcast.84, s32[131072]{0:T(1024)S(1)} %copy-done, f32[]{:T(128)} %bitcast.80), kind=kLoop, calls=%fused_computation.30 | loop fusion | flops 2490367 | bytes 4718600 | tf_op jit(solution)/shard_map/reduce_sum | solution.py:109
  125.8 62.6 %all-reduce = (f32[]{:T(128)}, f32[]{:T(128)}) all-reduce(f32[]{:T(128)} %get-tuple-element.16, f32[]{:T(128)} %fusion.24), channel_id=1, replica_groups=mesh['gx'=2,'gy'=4,'gz'=16] {'gx','gy','gz'}, use_global_device_ids=true, to_apply=%region_1.0 | all-reduce | flops 2 | bytes 16 | tf_op jit(solution)/shard_map/psum | solution.py:110
  (2 shorter events, 0.0 us)
Async XLA Ops:
  16.8 42.0 %all-to-all-start = ((f32[4,128,1024]{2,0,1:T(4,128)}), f32[4,128,1024]{2,0,1:T(4,128)}, u32[]{:S(2)}, u32[]{:S(2)}) async-start(f32[4,128,1024]{2,0,1:T(4,128)} %copy.17), calls=%async_computation | async-start | bytes 4194304 | tf_op jit(solution)/shard_map/all_to_all | solution.py:69
  70.6 35.5 %all-to-all-start.1 = ((f32[4,128,1024]{2,0,1:T(4,128)}), f32[4,128,1024]{2,0,1:T(4,128)}, u32[]{:S(2)}, u32[]{:S(2)}) async-start(f32[4,128,1024]{2,0,1:T(4,128)} %copy.19), calls=%async_computation.1 | async-start | bytes 4194304 | tf_op jit(solution)/shard_map/all_to_all | solution.py:106
  121.0 1.0 copy-start
where the time goes:
time: 193 us; the launch traced here: 192 us
  blocking collectives  62.6 us (32%)
  waiting for transfers between devices  58 us (30%)
  matrix products  24.2 us (13%)
  starting transfers between devices  17.3 us (9%)
  local copies, waits for them, and re-layouts  17.1 us (9%)
  other arithmetic  7.24 us (4%)
  between operations  5.65 us (3%)
    psum x1, blocking collectives, per_device(): gamma_total = lax.psum(gamma_part, ('gx', 'gy', 'gz'))  62.6 us
    all_to_all x1, waiting for transfers between devices, per_device(): lax.all_to_all(transformed.reshape(4, devices, row_size), ('gx', 'gy', 'g...  29.4 us
    all_to_all x1, waiting for transfers between devices, per_device(): lax.all_to_all(unspun, ('gx', 'gy', 'gz'), split_axis=1, concat_axis=1, t...  28.6 us
    all_to_all x1, starting transfers between devices, per_device(): lax.all_to_all(transformed.reshape(4, devices, row_size), ('gx', 'gy', 'g...  12 us
    dot_general x4, matrix products, walsh_local(): jnp.einsum('pakl,km->paml', shaped, matrix, precision=lax.Precision.HIGHE...  10.7 us
    dot_general x2, matrix products, walsh_local(): jnp.einsum('pak,km->pam', shaped, matrix, precision=lax.Precision.HIGHEST...  6.94 us
    another operation x2, local copies, waits for them, and re-layouts, per_device(): transformed.reshape(4, devices, row_size)  5.8 us
    all_to_all x1, starting transfers between devices, per_device(): lax.all_to_all(unspun, ('gx', 'gy', 'gz'), split_axis=1, concat_axis=1, t...  5.28 us
  transfers between devices with their start and end apart: 2, of which 2 were waited for; matrix products, arithmetic and copies ran while one was open for 1% of the time, Pallas kernels for 0%

commit v1 on v0

v1 whole, which is shorter than its diff:
```python
import functools
import math

import jax
import jax.numpy as jnp
from jax import lax
from jax.experimental import pallas as pl
from jax.experimental.pallas import tpu as pltpu
from jax.sharding import PartitionSpec as P


MESH = pl.DeviceIdType.MESH
AXES = ("gx", "gy", "gz")
PARTS = (((0, 4), (4, 4), (8, 3)), ((11, 4), (15, 4), (19, 3)), ((22, 4), (26, 3), (29, 3)))
STEPS = 3


def sincos(angle):
    turns = jnp.floor(angle * jnp.float32(2.0 / math.pi) + 0.5)
    rest = angle - turns * jnp.float32(1.5703125)
    rest = rest - turns * jnp.float32(4.837512969970703125e-4)
    rest = rest - turns * jnp.float32(7.54978995489188216e-8)
    square = rest * rest
    sine = ((-1.9515295891e-4 * square + 8.3321608736e-3) * square - 1.6666654611e-1) * square * rest + rest
    cosine = (
        ((2.443315711809948e-5 * square - 1.388731625493765e-3) * square + 4.166664568298827e-2) * square * square
        - 0.5 * square
        + 1.0
    )
    quadrant = turns - 4.0 * jnp.floor(turns * 0.25)
    odd = (quadrant == 1.0) | (quadrant == 3.0)
    sine_out = jnp.where(odd, cosine, sine)
    cosine_out = jnp.where(odd, sine, cosine)
    sine_out = jnp.where(quadrant >= 2.0, -sine_out, sine_out)
    cosine_out = jnp.where((quadrant == 1.0) | (quadrant == 2.0), -cosine_out, cosine_out)
    return sine_out, cosine_out


def inner(a, s):
    return a[0] * s[1] - a[1] * s[0]


def add(u, v):
    return u[0] + v[0], u[1] + v[1]


def turn(c, s, own, other):
    return c * own[0] - s * other[1], c * own[1] + s * other[0]


def mix_four(cc, ss, sc, x):
    outer, middle = add(x[0], x[3]), add(x[1], x[2])
    outer_re, outer_im = sc * outer[0], sc * outer[1]
    middle_re, middle_im = sc * middle[0], sc * middle[1]
    y = []
    for own, far, near_re, near_im in (
        (x[0], x[3], middle_re, middle_im),
        (x[1], x[2], outer_re, outer_im),
        (x[2], x[1], outer_re, outer_im),
        (x[3], x[0], middle_re, middle_im),
    ):
        y.append((cc * own[0] - ss * far[0] - near_im, cc * own[1] - ss * far[1] + near_re))
    return y, outer, middle


def kernel(
    gamma_ref, beta_ref, sr, si, ar, ai, energy_hbm,
    o0, o1, o2, o3, gamma_out, beta_out,
    mid, home, other, home_b, local_in, energy, trig, outs, consts, lane_u, lane_a, total, relay, landed,
    t_send, t_recv, r_send, r_recv, c_send, c_recv, in_sem, out_sem, red_send, red_recv,
):
    gx, gy, gz = (lax.axis_index(name) for name in AXES)
    x_lo, z, core = gz // 8, (gz // 2) % 4, gz % 2
    flip_core = gz + 1 - 2 * core

    def flips(v):
        return v, v + 1 - 2 * (v % 2), v + 2 - 4 * (v // 2), 3 - v

    place = (2 * gx + x_lo, gy, z)
    blocks = tuple(flips(v) for v in place)
    x_flip = gz + 8 - 16 * x_lo
    peers = (
        (None, (gx, gy, x_flip), (1 - gx, gy, gz), (1 - gx, gy, x_flip)),
        (None,) + tuple((gx, blocks[1][k], gz) for k in (1, 2, 3)),
        (None,) + tuple((gx, gy, gz + 2 * (blocks[2][k] - z)) for k in (1, 2, 3)),
    )
    core_peer = (gx, gy, flip_core)
    group = []
    for k in range(4):
        base = gz + 2 * (blocks[2][k] - z)
        group += [(gx, gy, base), (gx, gy, base + 1 - 2 * core)]

    ins = (sr, si, ar, ai)

    loads = []
    for i, ref in enumerate(ins):
        loads.append(pltpu.make_async_copy(ref, local_in.at[i], in_sem.at[i]))
    loads.append(pltpu.make_async_copy(energy_hbm, energy, in_sem.at[4]))

    barrier = pltpu.get_barrier_semaphore()
    greeted = list(peers[0][1:]) + list(peers[1][1:]) + group[1:]
    for device in greeted:
        pl.semaphore_signal(barrier, inc=1, device_id=device, device_id_type=MESH)
    pl.semaphore_wait(barrier, len(greeted))

    def send(src, dst, send_sem, recv_sem, device):
        pltpu.make_async_remote_copy(
            src_ref=src, dst_ref=dst, send_sem=send_sem, recv_sem=recv_sem, device_id=device, device_id_type=MESH
        ).start()

    def wait_bytes(ref, sem):
        pltpu.make_async_copy(ref, ref, sem).wait()

    def start_there(f, p, j):
        axis = (p + f) % 3
        r0, n = PARTS[p][j]
        me, rows = place[axis], pl.ds(r0, n)
        ss, rs = t_send.at[f, 3 * p + j], t_recv.at[f, 3 * p + j]
        for k in (3, 1, 2):
            block = blocks[axis][k]
            if f == 0:
                for i, ref in enumerate(ins):
                    send(ref.at[block, rows], mid.at[f, me, i, rows], ss, rs, peers[axis][k])
            else:
                src = (home_b if f == 1 else home.at[1]).at[block, :, rows]
                send(src, mid.at[f, me, :, rows], ss, rs, peers[axis][k])
        if f == 0:
            for i, ref in enumerate(ins):
                pltpu.make_async_copy(ref.at[me, rows], mid.at[f, me, i, rows], rs).start()
        else:
            src = (home_b if f == 1 else home.at[1]).at[me, :, rows]
            pltpu.make_async_copy(src, mid.at[f, me, :, rows], rs).start()

    def start_back(f, p, j):
        axis = (p + f) % 3
        r0, n = PARTS[p][j]
        me, rows = place[axis], pl.ds(r0, n)
        ss, rs = r_send.at[f, 3 * p + j], r_recv.at[f, 3 * p + j]
        for k in (3, 1, 2):
            block = blocks[axis][k]
            send(mid.at[f, block, :, rows], home.at[f, me, :, rows], ss, rs, peers[axis][k])
        pltpu.make_async_copy(mid.at[f, me, :, rows], home.at[f, me, :, rows], rs).start()

    def wait_there(f, p, j):
        rows = pl.ds(*PARTS[p][j])
        wait_bytes(mid.at[f, :, :, rows], t_recv.at[f, 3 * p + j])

    def wait_back(f, p, j):
        rows = pl.ds(*PARTS[p][j])
        wait_bytes(home.at[f, :, :, rows], r_recv.at[f, 3 * p + j])

    def wait_sent(f, p, j):
        rows = pl.ds(*PARTS[p][j])
        wait_bytes(mid.at[f, pl.ds(0, 3), :, rows], t_send.at[f, 3 * p + j])
        wait_bytes(mid.at[f, pl.ds(0, 3), :, rows], r_send.at[f, 3 * p + j])

    zero = jnp.zeros((8, 128), jnp.float32)

    def mix_axis(f, p, j):
        r0, n = PARTS[p][j]
        cc, ss, sc = consts[0], consts[1], consts[2]

        def body(r, acc):
            x = [[(mid[f, b, 2 * v, r], mid[f, b, 2 * v + 1, r]) for b in range(4)] for v in range(2)]
            s, s_outer, s_middle = mix_four(cc, ss, sc, x[0])
            a, a_outer, a_middle = mix_four(cc, ss, sc, x[1])
            for v, y in ((0, s), (1, a)):
                for b in range(4):
                    mid[f, b, 2 * v, r] = y[b][0]
                    mid[f, b, 2 * v + 1, r] = y[b][1]
            return acc + inner(a_outer, s_middle) + inner(a_middle, s_outer)

        total[1] += lax.fori_loop(r0, r0 + n, body, zero)

    def mix_core_and_blocks(p, j):
        r0, n = PARTS[p][j]
        cc, ss, sc, c, sn = (consts[i] for i in range(5))

        def body(r, acc):
            x = []
            for v in range(2):
                x.append([])
                for b in range(4):
                    own = home[0, b, 2 * v, r], home[0, b, 2 * v + 1, r]
                    far = other[b, 2 * v, r], other[b, 2 * v + 1, r]
                    if v == 0:
                        x[v].append((own, far))
                    else:
                        acc = acc + inner(own, x[0][b][1])
                        x[v].append((own, far))
            x = [[turn(c, sn, own, far) for own, far in half] for half in x]
            s, s_outer, s_middle = mix_four(cc, ss, sc, x[0])
            a, a_outer, a_middle = mix_four(cc, ss, sc, x[1])
            for v, y in ((0, s), (1, a)):
                for b in range(4):
                    home_b[b, 2 * v, r] = y[b][0]
                    home_b[b, 2 * v + 1, r] = y[b][1]
            return acc + inner(a_outer, s_middle) + inner(a_middle, s_outer)

        total[1] += lax.fori_loop(r0, r0 + n, body, zero)

    sub = lax.broadcasted_iota(jnp.int32, (8, 128), 0)

    def far_row(x, bit):
        step = 1 << bit
        if bit == 2:
            return pltpu.roll(x, 4, 0)
        return jnp.where((sub >> bit) & 1 == 1, pltpu.roll(x, step, 0), pltpu.roll(x, 8 - step, 0))

    def mix_lanes(p, j):
        r0, n = PARTS[p][j]
        rows = pl.ds(r0, n)
        c, sn = consts[3], consts[4]
        acc = zero
        for b in range(4):
            pair = []
            for v in range(2):
                re = home[1, b, 2 * v, rows].reshape(n * 8, 128)
                im = home[1, b, 2 * v + 1, rows].reshape(n * 8, 128)
                pair.append(jnp.concatenate([re, im], axis=1))
            both = jnp.concatenate(pair, axis=0)
            near = jnp.dot(
                pair[0], lane_a[...], precision=lax.Precision.HIGHEST, preferred_element_type=jnp.float32
            )
            part = inner((pair[1][:, :128], pair[1][:, 128:]), (near[:, :128], near[:, 128:]))
            acc = acc + jnp.sum(part.reshape(n, 8, 128), axis=0)
            mixed = jnp.dot(
                both, lane_u[...], precision=lax.Precision.HIGHEST, preferred_element_type=jnp.float32
            )
            for v in range(2):
                home[1, b, 2 * v, rows] = mixed[v * n * 8 : (v + 1) * n * 8, :128].reshape(n, 8, 128)
                home[1, b, 2 * v + 1, rows] = mixed[v * n * 8 : (v + 1) * n * 8, 128:].reshape(n, 8, 128)

        def body(i, acc):
            b, r = i // n, r0 + i % n
            s = home[1, b, 0, r], home[1, b, 1, r]
            a = home[1, b, 2, r], home[1, b, 3, r]
            for bit in range(3):
                s_far = far_row(s[0], bit), far_row(s[1], bit)
                a_far = far_row(a[0], bit), far_row(a[1], bit)
                acc = acc + inner(a, s_far)
                s = turn(c, sn, s, s_far)
                a = turn(c, sn, a, a_far)
            home[1, b, 0, r] = s[0]
            home[1, b, 1, r] = s[1]
            home[1, b, 2, r] = a[0]
            home[1, b, 3, r] = a[1]
            return acc

        total[1] += lax.fori_loop(0, 4 * n, body, acc)

    for j in range(STEPS):
        for p in range(3):
            start_there(0, p, j)
    for load in loads:
        load.start()

    sn, c = sincos(jnp.full((8, 128), beta_ref[0], jnp.float32))
    consts[0] = c * c
    consts[1] = sn * sn
    consts[2] = sn * c
    consts[3] = c
    consts[4] = sn
    consts[5] = sn / c
    consts[6] = c * c * c * c * c
    total[0] = zero
    total[1] = zero

    def build_lanes():
        c_row, s_row = consts[3], consts[4]

        def body(i, carry):
            row = lax.broadcasted_iota(jnp.int32, (8, 128), 0) + 8 * i
            bits = row ^ lax.broadcasted_iota(jnp.int32, (8, 128), 1)
            size = jnp.ones((8, 128), jnp.float32)
            ones = jnp.zeros((8, 128), jnp.int32)
            for bit in range(7):
                on = (bits >> bit) & 1
                size = size * jnp.where(on == 1, s_row, c_row)
                ones = ones + on
            real = jnp.where(ones % 4 == 0, size, jnp.where(ones % 4 == 2, -size, 0.0))
            imag = jnp.where(ones % 4 == 1, size, jnp.where(ones % 4 == 3, -size, 0.0))
            near = jnp.where(ones == 1, 1.0, 0.0)
            upper = pl.ds(pl.multiple_of(8 * i, 8), 8)
            lower = pl.ds(pl.multiple_of(128 + 8 * i, 8), 8)
            lane_u[upper, :128] = real
            lane_u[upper, 128:] = imag
            lane_u[lower, :128] = -imag
            lane_u[lower, 128:] = real
            lane_a[upper, :128] = near
            lane_a[upper, 128:] = jnp.zeros((8, 128), jnp.float32)
            lane_a[lower, :128] = jnp.zeros((8, 128), jnp.float32)
            lane_a[lower, 128:] = near
            return carry

        lax.fori_loop(0, 16, body, 0)

    def build_trig():
        gamma = gamma_ref[0]

        def body(i, carry):
            b, r = i // 32, i % 32
            sine, cosine = sincos(gamma * energy[b, r].astype(jnp.float32))
            trig[0, b, r] = cosine * consts[6]
            trig[1, b, r] = sine * consts[6]
            return carry

        lax.fori_loop(0, 128, body, 0)

    def tile_bits_derivative():
        def body(i, acc):
            b, r = i // 32, i % 32
            near_re, near_im = zero, zero
            for bit in range(5):
                far = r + (1 << bit) - (2 << bit) * ((r // (1 << bit)) % 2)
                near_re = near_re + local_in[0, b, far]
                near_im = near_im + local_in[1, b, far]
            return acc + inner((local_in[2, b, r], local_in[3, b, r]), (near_re, near_im))

        total[1] += lax.fori_loop(0, 128, body, zero)

    build_lanes()
    for j in range(STEPS):
        for p in range(3):
            wait_there(0, p, j)
            mix_axis(0, p, j)
            start_back(0, p, j)
        if j == 0:
            for load in loads:
                load.wait()
            build_trig()
        if j == 1:
            tile_bits_derivative()

    for j in range(STEPS):
        for p in range(3):
            rows = pl.ds(*PARTS[p][j])
            wait_back(0, p, j)
            send(home.at[0, :, :, rows], other.at[:, :, rows], c_send.at[3 * p + j], c_recv.at[3 * p + j], core_peer)
        for p in range(3):
            rows = pl.ds(*PARTS[p][j])
            wait_bytes(other.at[:, :, rows], c_recv.at[3 * p + j])
            mix_core_and_blocks(p, j)
            start_there(1, p, j)
    for j in range(STEPS):
        for p in range(3):
            wait_there(1, p, j)
            mix_axis(1, p, j)
            start_back(1, p, j)
    for j in range(STEPS):
        for p in range(3):
            wait_back(1, p, j)
            mix_lanes(p, j)
            start_there(2, p, j)
    for j in range(STEPS):
        for p in range(3):
            wait_there(2, p, j)
            mix_axis(2, p, j)
            start_back(2, p, j)
    for j in range(STEPS):
        for p in range(3):
            rows = pl.ds(*PARTS[p][j])
            wait_sent(0, p, j)
            wait_sent(1, p, j)
            wait_bytes(other.at[:, :, rows], c_send.at[3 * p + j])
    for j in range(STEPS):
        for p in range(3):
            wait_back(2, p, j)

    t = consts[5]

    def tile_pair(u, v):
        return (
            (u[0] - t * v[1], u[1] + t * v[0]),
            (v[0] - t * u[1], v[1] + t * u[0]),
        )

    def low_bits(i, carry):
        b, first = i // 4, 8 * (i % 4)
        for v in range(2):
            x = [(home[2, b, 2 * v, first + k], home[2, b, 2 * v + 1, first + k]) for k in range(8)]
            for bit in range(3):
                for k in range(8):
                    if not k >> bit & 1:
                        x[k], x[k + (1 << bit)] = tile_pair(x[k], x[k + (1 << bit)])
            for k in range(8):
                home[2, b, 2 * v, first + k] = x[k][0]
                home[2, b, 2 * v + 1, first + k] = x[k][1]
        return carry

    def high_bits(b, i, acc):
        ys = []
        for v in range(2):
            x = [(home[2, b, 2 * v, 8 * k + i], home[2, b, 2 * v + 1, 8 * k + i]) for k in range(4)]
            x[0], x[1] = tile_pair(x[0], x[1])
            x[2], x[3] = tile_pair(x[2], x[3])
            x[0], x[2] = tile_pair(x[0], x[2])
            x[1], x[3] = tile_pair(x[1], x[3])
            ys.append(x)
        for k in range(4):
            r = 8 * k + i
            cosine, sine = trig[0, b, r], trig[1, b, r]
            s, a = ((y[k][0] * cosine - y[k][1] * sine, y[k][0] * sine + y[k][1] * cosine) for y in ys)
            outs[0, b, r] = s[0]
            outs[1, b, r] = s[1]
            outs[2, b, r] = a[0]
            outs[3, b, r] = a[1]
            acc = acc + energy[b, r].astype(jnp.float32) * inner(a, s)
        return acc

    lax.fori_loop(0, 16, low_bits, 0)
    acc = zero
    results = (o0, o1, o2, o3)
    for b in range(4):
        acc = lax.fori_loop(0, 8, functools.partial(high_bits, b), acc)
        for i in range(4):
            pltpu.make_async_copy(outs.at[i, b], results[i].at[b], out_sem.at[i, b]).start()
    total[0] = acc

    relay[0] = total[...]
    slot = 0
    for stage, (targets, first) in enumerate(((peers[0][1:], 0), (peers[1][1:], 3), (group[1:], 6))):
        count = len(targets)
        for k, device in enumerate(targets):
            send(relay.at[stage], landed.at[first + k], red_send.at[stage], red_recv.at[stage], device)
        if stage == 0:
            for j in range(STEPS):
                for p in range(3):
                    wait_sent(2, p, j)
        wait_bytes(landed.at[pl.ds(first, count)], red_recv.at[stage])
        terms = [relay[stage]] + [landed[first + k] for k in range(count)]
        while len(terms) > 1:
            terms = [terms[i] + terms[i + 1] for i in range(0, len(terms), 2)]
        relay[stage + 1] = terms[0]
    scale = jnp.float32(1.0 / 16777216.0)
    gamma_out[0] = jnp.sum(relay[3, 0]) * scale
    beta_out[0] = jnp.sum(relay[3, 1]) * scale
    for stage, count in ((0, 3), (1, 3), (2, 7)):
        wait_bytes(landed.at[pl.ds(0, count)], red_send.at[stage])
    for b in range(4):
        for i in range(4):
            pltpu.make_async_copy(outs.at[i, b], results[i].at[b], out_sem.at[i, b]).wait()


def per_device(state_real, state_imag, adjoint_real, adjoint_imag, energies, gamma_angle, beta_angle):
    shape = (4, 32, 8, 128)
    args = [v.reshape(shape) for v in (state_real, state_imag, adjoint_real, adjoint_imag, energies)]
    hbm = pl.BlockSpec(memory_space=pl.ANY)
    smem = pl.BlockSpec(memory_space=pltpu.SMEM)
    f32 = jnp.float32
    dma = pltpu.SemaphoreType.DMA
    big = jax.ShapeDtypeStruct(shape, f32)
    one = jax.ShapeDtypeStruct((1,), f32)
    results = pl.pallas_call(
        kernel,
        out_shape=(big, big, big, big, one, one),
        in_specs=[smem, smem] + [hbm] * 5,
        out_specs=(hbm, hbm, hbm, hbm, smem, smem),
        scratch_shapes=[
            pltpu.VMEM((3, 4, 4, 32, 8, 128), f32),
            pltpu.VMEM((3, 4, 4, 32, 8, 128), f32),
            pltpu.VMEM((4, 4, 32, 8, 128), f32),
            pltpu.VMEM((4, 4, 32, 8, 128), f32),
            pltpu.VMEM((4, 4, 32, 8, 128), f32),
            pltpu.VMEM(shape, jnp.int32),
            pltpu.VMEM((2,) + shape, f32),
            pltpu.VMEM((4,) + shape, f32),
            pltpu.VMEM((7, 8, 128), f32),
            pltpu.VMEM((256, 256), f32),
            pltpu.VMEM((256, 256), f32),
            pltpu.VMEM((2, 8, 128), f32),
            pltpu.VMEM((4, 2, 8, 128), f32),
            pltpu.VMEM((13, 2, 8, 128), f32),
            dma((3, 9)),
            dma((3, 9)),
            dma((3, 9)),
            dma((3, 9)),
            dma((9,)),
            dma((9,)),
            dma((5,)),
            dma((4, 4)),
            dma((3,)),
            dma((3,)),
        ],
        compiler_params=pltpu.CompilerParams(
            collective_id=0, has_side_effects=True, vmem_limit_bytes=50 << 20
        ),
        cost_estimate=pl.CostEstimate(flops=2 << 30, bytes_accessed=5 << 20, transcendentals=0),
    )(gamma_angle, beta_angle, *args)
    return tuple(v.reshape(-1) for v in results[:4]) + (results[4], results[5])


def solution(mesh):
    whole = P(AXES)
    return jax.shard_map(
        per_device,
        mesh=mesh,
        in_specs=(whole,) * 5 + (P(), P()),
        out_specs=(whole,) * 4 + (P(), P()),
        check_vma=False,
    )
```

time: 193 us -> 93.8 us (0.49)
  Pallas kernels: 0 us -> 81.6 us
  blocking collectives: 62.6 us -> 0 us
  waiting for transfers between devices: 58 us -> 0 us
  matrix products: 24.2 us -> 0 us
  starting transfers between devices: 17.3 us -> 0 us
  local copies, waits for them, and re-layouts: 17.1 us -> 6.43 us
  other arithmetic: 7.24 us -> 0 us
    pallas_call x0 -> x1, Pallas kernels: none -> 81.6 us  [per_device(): pl.pallas_call(kernel, out_shape=(big, big, big, big, one, one), in_specs...]
    psum x1 -> x0, blocking collectives: 62.6 us -> none  [per_device(): gamma_total = lax.psum(gamma_part, ('gx', 'gy', 'gz'))]
    all_to_all x2 -> x0, waiting for transfers between devices: 58 us -> none  [the longest x1 29.4 us: per_device(): lax.all_to_all(transformed.reshape(4, devices, row_size), ('gx', 'gy', 'g...]
    dot_general x8 -> x0, matrix products: 24.2 us -> none  [the longest x4 10.7 us: walsh_local(): jnp.einsum('pakl,km->paml', shaped, matrix, precision=lax.Precision.HIGHE...]
    all_to_all x2 -> x0, starting transfers between devices: 17.3 us -> none  [the longest x1 12 us: per_device(): lax.all_to_all(transformed.reshape(4, devices, row_size), ('gx', 'gy', 'g...]
    another operation x3 -> x0, local copies, waits for them, and re-layouts: 7.36 us -> none  [the longest x2 5.8 us: per_device(): transformed.reshape(4, devices, row_size)]
    unnamed x7 -> x10, local copies, waits for them, and re-layouts: 1.14 us -> 6.43 us
    reduce_sum x2 -> x0, other arithmetic: 4.71 us -> none  [the longest x1 3.74 us: per_device(): jnp.sum(energy_float * (middle[2] * middle[1] - middle[3] * middle[0]))]
  transfers between devices with their start and end apart: 2 -> 0, of which waited for: 2 -> 0; matrix products, arithmetic and copies ran while one was open for 1% -> 0% of each run, Pallas kernels for 0% -> 0%
where the time goes in v1:
time: 93.8 us; the launch traced here: 93.5 us
  Pallas kernels  81.6 us (87%)
  local copies, waits for them, and re-layouts  6.43 us (7%)
  between operations  5.43 us (6%)
    pallas_call x1, Pallas kernels, per_device(): pl.pallas_call(kernel, out_shape=(big, big, big, big, one, one), in_specs...  81.6 us
    unnamed x10, local copies, waits for them, and re-layouts  6.43 us

profile of v1, /device:TPU:1, one launch (start us, length us, event | category | flops | bytes accessed | tf_op | source)
XLA Modules:
  0.0 93.5 jit_solution(8477815176145049977)
XLA Ops:
  1.9 0.0 copy-start
  1.9 1.0 %copy-done = f32[131072]{0:T(1024)S(1)} copy-done((f32[131072]{0:T(1024)S(1)}, f32[131072]{0:T(1024)}, u32[]{:S(2)}) %copy-start) | copy-done | bytes 524312
  3.0 0.0 copy-start.1
  3.0 1.0 %copy-done.1 = f32[131072]{0:T(1024)S(1)} copy-done((f32[131072]{0:T(1024)S(1)}, f32[131072]{0:T(1024)}, u32[]{:S(2)}) %copy-start.1) | copy-done | bytes 524312
  4.0 0.0 copy-start.2
  4.0 1.0 %copy-done.2 = f32[131072]{0:T(1024)S(1)} copy-done((f32[131072]{0:T(1024)S(1)}, f32[131072]{0:T(1024)}, u32[]{:S(2)}) %copy-start.2) | copy-done | bytes 524312
  5.1 81.6 %shard_map.118 = (f32[4,32,8,128]{3,2,1,0:T(8,128)S(1)}, f32[4,32,8,128]{3,2,1,0:T(8,128)S(1)}, f32[4,32,8,128]{3,2,1,0:T(8,128)S(1)}, f32[4,32,8,128]{3,2,1,0:T(8,128)S(1)}, f32[1]{0:T(128)}, /*index=5*/f32[1]{0:T(128)}) custom-call(f32[1]{0:T(128)S(6)} %copy.19.gamma_ref, f32[1]{0:T(128)S(6)} %copy.20.beta_ref, f32[4,32,8,128]{3,2,1,0:T(8,128)S(1)} %bitcast.13, ...), custom_call_target="tpu_custom_call" | custom-call | flops 2147483648 | bytes 5242880 | tf_op jit(solution)/shard_map/pallas_call | solution.py:454
  86.7 0.8 copy.21
  87.5 0.8 copy.22
  88.3 0.8 copy.23
  89.1 0.8 copy.24
Async XLA Ops:
  1.9 1.0 %copy-start = (f32[131072]{0:T(1024)S(1)}, f32[131072]{0:T(1024)}, u32[]{:S(2)}) copy-start(f32[131072]{0:T(1024)} %param.7) | copy-start | bytes 1572868
  3.0 1.0 %copy-start.1 = (f32[131072]{0:T(1024)S(1)}, f32[131072]{0:T(1024)}, u32[]{:S(2)}) copy-start(f32[131072]{0:T(1024)} %param.8) | copy-start | bytes 1572868
  4.0 1.0 %copy-start.2 = (f32[131072]{0:T(1024)S(1)}, f32[131072]{0:T(1024)}, u32[]{:S(2)}) copy-start(f32[131072]{0:T(1024)} %param.9) | copy-start | bytes 1572868

commit v2 on v1

v2 whole, which is shorter than its diff:
```python
import functools
import math

import jax
import jax.numpy as jnp
from jax import lax
from jax.experimental import pallas as pl
from jax.experimental.pallas import tpu as pltpu
from jax.sharding import PartitionSpec as P


MESH = pl.DeviceIdType.MESH
AXES = ("gx", "gy", "gz")
STEPS = 3
EARLY = 1


def cut(first, count):
    sizes = [count // STEPS + (i < count % STEPS) for i in range(STEPS)]
    return tuple((first + sum(sizes[:i]), sizes[i]) for i in range(STEPS))


PARTS = (cut(0, 11), cut(11, 11), cut(22, 10))


def sincos(angle):
    turns = jnp.floor(angle * jnp.float32(2.0 / math.pi) + 0.5)
    rest = angle - turns * jnp.float32(1.5703125)
    rest = rest - turns * jnp.float32(4.837512969970703125e-4)
    rest = rest - turns * jnp.float32(7.54978995489188216e-8)
    square = rest * rest
    sine = ((-1.9515295891e-4 * square + 8.3321608736e-3) * square - 1.6666654611e-1) * square * rest + rest
    cosine = (
        ((2.443315711809948e-5 * square - 1.388731625493765e-3) * square + 4.166664568298827e-2) * square * square
        - 0.5 * square
        + 1.0
    )
    quadrant = turns - 4.0 * jnp.floor(turns * 0.25)
    odd = (quadrant == 1.0) | (quadrant == 3.0)
    sine_out = jnp.where(odd, cosine, sine)
    cosine_out = jnp.where(odd, sine, cosine)
    sine_out = jnp.where(quadrant >= 2.0, -sine_out, sine_out)
    cosine_out = jnp.where((quadrant == 1.0) | (quadrant == 2.0), -cosine_out, cosine_out)
    return sine_out, cosine_out


def inner(a, s):
    return a[0] * s[1] - a[1] * s[0]


def add(u, v):
    return u[0] + v[0], u[1] + v[1]


def turn(c, s, own, other):
    return c * own[0] - s * other[1], c * own[1] + s * other[0]


def mix_four(cc, ss, sc, x):
    outer, middle = add(x[0], x[3]), add(x[1], x[2])
    outer_re, outer_im = sc * outer[0], sc * outer[1]
    middle_re, middle_im = sc * middle[0], sc * middle[1]
    y = []
    for own, far, near_re, near_im in (
        (x[0], x[3], middle_re, middle_im),
        (x[1], x[2], outer_re, outer_im),
        (x[2], x[1], outer_re, outer_im),
        (x[3], x[0], middle_re, middle_im),
    ):
        y.append((cc * own[0] - ss * far[0] - near_im, cc * own[1] - ss * far[1] + near_re))
    return y, outer, middle


def kernel(
    gamma_ref, beta_ref, sr, si, ar, ai, energy_hbm,
    o0, o1, o2, o3, gamma_out, beta_out,
    mid, home, other, home_b, local_in, energy, energy_mid, trig, consts, lane_u, lane_a, total, relay, landed,
    t_send, t_recv, r_send, r_recv, c_send, c_recv, e_send, e_recv, in_sem, red_send, red_recv,
):
    gx, gy, gz = (lax.axis_index(name) for name in AXES)
    x_lo, z, core = gz // 8, (gz // 2) % 4, gz % 2
    flip_core = gz + 1 - 2 * core

    def flips(v):
        return v, v + 1 - 2 * (v % 2), v + 2 - 4 * (v // 2), 3 - v

    place = (2 * gx + x_lo, gy, z)
    blocks = tuple(flips(v) for v in place)
    x_flip = gz + 8 - 16 * x_lo
    peers = (
        (None, (gx, gy, x_flip), (1 - gx, gy, gz), (1 - gx, gy, x_flip)),
        (None,) + tuple((gx, blocks[1][k], gz) for k in (1, 2, 3)),
        (None,) + tuple((gx, gy, gz + 2 * (blocks[2][k] - z)) for k in (1, 2, 3)),
    )
    core_peer = (gx, gy, flip_core)
    group = []
    for k in range(4):
        base = gz + 2 * (blocks[2][k] - z)
        group += [(gx, gy, base), (gx, gy, base + 1 - 2 * core)]

    plane = []
    for i in range(4):
        over, along = ((gx, gz), (gx, x_flip), (1 - gx, gz), (1 - gx, x_flip))[i]
        plane += [(over, blocks[1][k], along) for k in range(4)]

    ins = (sr, si, ar, ai)

    loads = []
    for i, ref in enumerate(ins):
        loads.append(pltpu.make_async_copy(ref, local_in.at[:, i], in_sem.at[i]))
    loads.append(pltpu.make_async_copy(energy_hbm, energy, in_sem.at[4]))

    barrier = pltpu.get_barrier_semaphore()
    greeted = plane[1:] + group[1:]
    for device in greeted:
        pl.semaphore_signal(barrier, inc=1, device_id=device, device_id_type=MESH)
    for load in loads:
        load.start()

    def send(src, dst, send_sem, recv_sem, device):
        pltpu.make_async_remote_copy(
            src_ref=src, dst_ref=dst, send_sem=send_sem, recv_sem=recv_sem, device_id=device, device_id_type=MESH
        ).start()

    def wait_bytes(ref, sem):
        pltpu.make_async_copy(ref, ref, sem).wait()

    def start_there(f, p, j):
        axis = (p + f) % 3
        r0, n = PARTS[p][j]
        me, rows = place[axis], pl.ds(r0, n)
        ss, rs = t_send.at[f, STEPS * p + j], t_recv.at[f, STEPS * p + j]
        source = (local_in, home_b, home.at[1])[f]
        for k in (2, 3, 1):
            send(source.at[blocks[axis][k], :, rows], mid.at[f, me, :, rows], ss, rs, peers[axis][k])
        pltpu.make_async_copy(source.at[me, :, rows], mid.at[f, me, :, rows], rs).start()

    def part_rows(p):
        return pl.ds(PARTS[p][0][0], sum(n for _, n in PARTS[p]))

    def start_energy(p):
        axis, rows = (p + 2) % 3, part_rows(p)
        me = place[axis]
        for k in (2, 3, 1):
            block = blocks[axis][k]
            send(energy_hbm.at[block, rows], energy_mid.at[me, rows], e_send.at[p], e_recv.at[p], peers[axis][k])
        pltpu.make_async_copy(energy_hbm.at[me, rows], energy_mid.at[me, rows], e_recv.at[p]).start()

    def wait_energy(p):
        wait_bytes(energy_mid.at[:, part_rows(p)], e_recv.at[p])
        wait_bytes(energy_mid.at[pl.ds(0, 3), part_rows(p)], e_send.at[p])

    def start_back(f, p, j):
        axis = (p + f) % 3
        r0, n = PARTS[p][j]
        me, rows = place[axis], pl.ds(r0, n)
        ss, rs = r_send.at[f, STEPS * p + j], r_recv.at[f, STEPS * p + j]
        for k in (2, 3, 1):
            block = blocks[axis][k]
            send(mid.at[f, block, :, rows], home.at[f, me, :, rows], ss, rs, peers[axis][k])
        pltpu.make_async_copy(mid.at[f, me, :, rows], home.at[f, me, :, rows], rs).start()

    def wait_there(f, p, j):
        rows = pl.ds(*PARTS[p][j])
        wait_bytes(mid.at[f, :, :, rows], t_recv.at[f, STEPS * p + j])

    def wait_back(f, p, j):
        rows = pl.ds(*PARTS[p][j])
        wait_bytes(home.at[f, :, :, rows], r_recv.at[f, STEPS * p + j])

    def wait_sent(f, p, j):
        rows = pl.ds(*PARTS[p][j])
        wait_bytes(mid.at[f, pl.ds(0, 3), :, rows], t_send.at[f, STEPS * p + j])
        wait_bytes(mid.at[f, pl.ds(0, 3), :, rows], r_send.at[f, STEPS * p + j])

    zero = jnp.zeros((8, 128), jnp.float32)

    sub = lax.broadcasted_iota(jnp.int32, (8, 128), 0)

    def far_row(x, bit):
        step = 1 << bit
        if bit == 2:
            return pltpu.roll(x, 4, 0)
        return jnp.where((sub >> bit) & 1 == 1, pltpu.roll(x, step, 0), pltpu.roll(x, 8 - step, 0))

    def mix_axis(f, p, j):
        r0, n = PARTS[p][j]
        cc, ss, sc = (consts[i + (5 if f == 0 else 0)] for i in range(3))
        c, sn = consts[3], consts[4]

        def body(r, accs):
            acc, acc_gamma = accs
            x = [[(mid[f, b, 2 * v, r], mid[f, b, 2 * v + 1, r]) for b in range(4)] for v in range(2)]
            s, s_outer, s_middle = mix_four(cc, ss, sc, x[0])
            a, a_outer, a_middle = mix_four(cc, ss, sc, x[1])
            acc = acc + inner(a_outer, s_middle) + inner(a_middle, s_outer)
            for b in range(4):
                if f == 1:
                    for bit in range(3):
                        s_far = far_row(s[b][0], bit), far_row(s[b][1], bit)
                        a_far = far_row(a[b][0], bit), far_row(a[b][1], bit)
                        acc = acc + inner(a[b], s_far)
                        s[b] = turn(c, sn, s[b], s_far)
                        a[b] = turn(c, sn, a[b], a_far)
                if f == 2:
                    acc_gamma = acc_gamma + energy_mid[b, r].astype(jnp.float32) * inner(a[b], s[b])
                mid[f, b, 0, r] = s[b][0]
                mid[f, b, 1, r] = s[b][1]
                mid[f, b, 2, r] = a[b][0]
                mid[f, b, 3, r] = a[b][1]
            return acc, acc_gamma

        acc, acc_gamma = lax.fori_loop(r0, r0 + n, body, (zero, zero))
        total[1] += acc * consts[8] if f == 0 else acc
        if f == 2:
            total[0] += acc_gamma

    def mix_core_and_blocks(p, j):
        r0, n = PARTS[p][j]
        cc, ss, sc, c, sn = (consts[i] for i in range(5))

        def body(r, acc):
            x = []
            for v in range(2):
                x.append([])
                for b in range(4):
                    own = home[0, b, 2 * v, r], home[0, b, 2 * v + 1, r]
                    far = other[b, 2 * v, r], other[b, 2 * v + 1, r]
                    if v == 0:
                        x[v].append((own, far))
                    else:
                        acc = acc + inner(own, x[0][b][1])
                        x[v].append((own, far))
            x = [[turn(c, sn, own, far) for own, far in half] for half in x]
            s, s_outer, s_middle = mix_four(cc, ss, sc, x[0])
            a, a_outer, a_middle = mix_four(cc, ss, sc, x[1])
            for v, y in ((0, s), (1, a)):
                for b in range(4):
                    home_b[b, 2 * v, r] = y[b][0]
                    home_b[b, 2 * v + 1, r] = y[b][1]
            return acc + inner(a_outer, s_middle) + inner(a_middle, s_outer)

        total[1] += lax.fori_loop(r0, r0 + n, body, zero)

    def mix_lanes(p, j):
        r0, n = PARTS[p][j]
        rows, size = pl.ds(r0, n), n * 8

        def halves(v):
            parts = []
            for b in range(4):
                re = home[1, b, 2 * v, rows].reshape(size, 128)
                im = home[1, b, 2 * v + 1, rows].reshape(size, 128)
                parts.append(jnp.concatenate([re, im], axis=1))
            full = jnp.concatenate(parts, axis=0)
            high = full.astype(jnp.bfloat16)
            return full, high, (full - high.astype(jnp.float32)).astype(jnp.bfloat16)

        dot = functools.partial(jnp.dot, preferred_element_type=jnp.float32)
        u_high, u_low, near = lane_u[0], lane_u[1], lane_a[...]
        _, s_high, s_low = halves(0)
        full, a_high, a_low = halves(1)
        s_near = dot(s_high, near) + dot(s_low, near)
        part = inner((full[:, :128], full[:, 128:]), (s_near[:, :128], s_near[:, 128:]))
        total[1] += jnp.sum(part.reshape(4 * n, 8, 128), axis=0)
        for v, (high, low) in enumerate(((s_high, s_low), (a_high, a_low))):
            mixed = dot(high, u_high) + (dot(low, u_high) + dot(high, u_low))
            for b in range(4):
                home[1, b, 2 * v, rows] = mixed[b * size : (b + 1) * size, :128].reshape(n, 8, 128)
                home[1, b, 2 * v + 1, rows] = mixed[b * size : (b + 1) * size, 128:].reshape(n, 8, 128)

    sn, c = sincos(jnp.full((8, 128), beta_ref[0], jnp.float32))
    scale_tiles = c * c * c * c * c
    tangent = sn / c
    for i, value in enumerate((c * c, sn * sn, sn * c, c, sn)):
        consts[i] = value
    for i in range(3):
        consts[5 + i] = consts[i] * scale_tiles
    consts[8] = scale_tiles * scale_tiles
    total[0] = zero
    total[1] = zero

    def tile_pair(u, v):
        return (
            (u[0] - tangent * v[1], u[1] + tangent * v[0]),
            (v[0] - tangent * u[1], v[1] + tangent * u[0]),
        )

    def mix_tiles(b, v, places, bits):
        x = [(local_in[b, 2 * v, r], local_in[b, 2 * v + 1, r]) for r in places]
        for bit in range(bits):
            for k in range(1 << bits):
                if not k >> bit & 1:
                    x[k], x[k + (1 << bit)] = tile_pair(x[k], x[k + (1 << bit)])
        for r, (re, im) in zip(places, x):
            local_in[b, 2 * v, r] = re
            local_in[b, 2 * v + 1, r] = im

    def low_bits(i, carry):
        for v in range(2):
            mix_tiles(i // 4, v, [8 * (i % 4) + k for k in range(8)], 3)
        return carry

    def high_bits(i, carry):
        for v in range(2):
            mix_tiles(i // 8, v, [i % 8 + 8 * k for k in range(4)], 2)
        return carry

    pl.semaphore_wait(barrier, len(greeted))
    for p in range(3):
        start_energy(p)
    for load in loads[:4]:
        load.wait()
    lax.fori_loop(0, 16, low_bits, 0)
    lax.fori_loop(0, 32, high_bits, 0)

    for j in range(STEPS):
        for p in range(3):
            start_there(0, p, j)
    loads[4].wait()

    def build_lanes():
        c_row, s_row = (jnp.concatenate([consts[i], consts[i]], axis=0) for i in (3, 4))

        def body(i, carry):
            row = lax.broadcasted_iota(jnp.int32, (16, 128), 0) + 16 * i
            bits = row ^ lax.broadcasted_iota(jnp.int32, (16, 128), 1)
            size = jnp.ones((16, 128), jnp.float32)
            ones = jnp.zeros((16, 128), jnp.int32)
            for bit in range(7):
                on = (bits >> bit) & 1
                size = size * jnp.where(on == 1, s_row, c_row)
                ones = ones + on
            real = jnp.where(ones % 4 == 0, size, jnp.where(ones % 4 == 2, -size, 0.0))
            imag = jnp.where(ones % 4 == 1, size, jnp.where(ones % 4 == 3, -size, 0.0))
            near = jnp.where(ones == 1, 1.0, 0.0).astype(jnp.bfloat16)
            upper = pl.ds(pl.multiple_of(16 * i, 16), 16)
            lower = pl.ds(pl.multiple_of(128 + 16 * i, 16), 16)
            for rows, left, right in ((upper, real, imag), (lower, -imag, real)):
                for columns, value in ((slice(0, 128), left), (slice(128, 256), right)):
                    high = value.astype(jnp.bfloat16)
                    lane_u[0, rows, columns] = high
                    lane_u[1, rows, columns] = (value - high.astype(jnp.float32)).astype(jnp.bfloat16)
            lane_a[upper, :128] = near
            lane_a[upper, 128:] = jnp.zeros_like(near)
            lane_a[lower, :128] = jnp.zeros_like(near)
            lane_a[lower, 128:] = near
            return carry

        lax.fori_loop(0, 8, body, 0)

    def build_trig():
        gamma = gamma_ref[0]

        def body(i, carry):
            b, r = i // 32, i % 32
            sine, cosine = sincos(gamma * energy[b, r].astype(jnp.float32))
            trig[0, b, r] = cosine
            trig[1, b, r] = sine
            return carry

        lax.fori_loop(0, 128, body, 0)

    def tile_bits_derivative():
        def body(i, acc):
            b, r = i // 32, i % 32
            near_re, near_im = zero, zero
            for bit in range(5):
                far = r + (1 << bit) - (2 << bit) * ((r // (1 << bit)) % 2)
                near_re = near_re + local_in[b, 0, far]
                near_im = near_im + local_in[b, 1, far]
            return acc + inner((local_in[b, 2, r], local_in[b, 3, r]), (near_re, near_im))

        total[1] += lax.fori_loop(0, 128, body, zero) * consts[8]

    build_lanes()
    build_trig()
    tile_bits_derivative()
    for j in range(STEPS):
        for p in range(3):
            wait_there(0, p, j)
            mix_axis(0, p, j)
            start_back(0, p, j)

    for j in range(STEPS):
        for p in range(3):
            rows = pl.ds(*PARTS[p][j])
            wait_back(0, p, j)
            send(home.at[0, :, :, rows], other.at[:, :, rows], c_send.at[STEPS * p + j], c_recv.at[STEPS * p + j], core_peer)
        for p in range(3):
            rows = pl.ds(*PARTS[p][j])
            wait_bytes(other.at[:, :, rows], c_recv.at[STEPS * p + j])
            mix_core_and_blocks(p, j)
            start_there(1, p, j)
    for j in range(STEPS):
        for p in range(3):
            wait_there(1, p, j)
            mix_axis(1, p, j)
            start_back(1, p, j)
    for j in range(STEPS):
        for p in range(3):
            wait_back(1, p, j)
            mix_lanes(p, j)
            start_there(2, p, j)
    for p in range(3):
        wait_energy(p)
    for j in range(STEPS):
        for p in range(3):
            wait_there(2, p, j)
            mix_axis(2, p, j)
            if j < EARLY:
                start_back(2, p, j)

    stages = ((group[1:], 0), (plane[1:], 7))
    results = (o0, o1, o2, o3)

    def start_sum(stage):
        targets, first = stages[stage]
        for k, device in enumerate(targets):
            send(relay.at[stage, :2], landed.at[first + k, :2], red_send.at[stage], red_recv.at[stage], device)

    def finish_sum(stage):
        targets, first = stages[stage]
        count = len(targets)
        wait_bytes(landed.at[pl.ds(first, count), :2], red_recv.at[stage])
        terms = [relay[stage, :2]] + [landed[first + k, :2] for k in range(count)]
        while len(terms) > 1:
            terms = [terms[i] + terms[i + 1] for i in range(0, len(terms), 2)]
        relay[stage + 1, :2] = terms[0]

    def turn_back(p, j):
        r0, n = PARTS[p][j]

        def body(r, carry):
            for b in range(4):
                cosine, sine = trig[0, b, r], trig[1, b, r]
                for v in range(2):
                    re, im = home[2, b, 2 * v, r], home[2, b, 2 * v + 1, r]
                    results[2 * v][b, r] = re * cosine - im * sine
                    results[2 * v + 1][b, r] = re * sine + im * cosine
            return carry

        lax.fori_loop(r0, r0 + n, body, 0)

    for i in range(2):
        relay[0, i : i + 1] = jnp.sum(total[i], axis=0, keepdims=True)
    start_sum(0)
    for j in range(EARLY, STEPS):
        for p in range(3):
            start_back(2, p, j)
    for j in range(STEPS):
        for p in range(3):
            rows = pl.ds(*PARTS[p][j])
            wait_sent(0, p, j)
            wait_sent(1, p, j)
            wait_bytes(other.at[:, :, rows], c_send.at[STEPS * p + j])
    for j in range(STEPS):
        for p in range(3):
            wait_back(2, p, j)
            turn_back(p, j)
        if j == 0:
            finish_sum(0)
            start_sum(1)
    for j in range(STEPS):
        for p in range(3):
            wait_sent(2, p, j)
    finish_sum(1)
    scale = jnp.float32(1.0 / 16777216.0)
    gamma_out[0] = jnp.sum(relay[2, 0:1]) * scale
    beta_out[0] = jnp.sum(relay[2, 1:2]) * scale
    for stage, count in ((0, 7), (1, 15)):
        wait_bytes(landed.at[pl.ds(0, count), :2], red_send.at[stage])


def store_kernel(i0, i1, i2, i3, o0, o1, o2, o3, sem):
    copies = [pltpu.make_async_copy(i, o, sem.at[k]) for k, (i, o) in enumerate(((i0, o0), (i1, o1), (i2, o2), (i3, o3)))]
    for copy in copies:
        copy.start()
    for copy in copies:
        copy.wait()


def per_device(state_real, state_imag, adjoint_real, adjoint_imag, energies, gamma_angle, beta_angle):
    shape = (4, 32, 8, 128)
    args = [v.reshape(shape) for v in (state_real, state_imag, adjoint_real, adjoint_imag, energies)]
    hbm = pl.BlockSpec(memory_space=pltpu.HBM)
    vmem = pl.BlockSpec(memory_space=pltpu.VMEM)
    smem = pl.BlockSpec(memory_space=pltpu.SMEM)
    f32 = jnp.float32
    dma = pltpu.SemaphoreType.DMA
    big = pltpu.VMEM(shape, f32)
    one = jax.ShapeDtypeStruct((1,), f32)
    results = pl.pallas_call(
        kernel,
        out_shape=(big, big, big, big, one, one),
        in_specs=[smem, smem] + [hbm] * 5,
        out_specs=(vmem, vmem, vmem, vmem, smem, smem),
        scratch_shapes=[
            pltpu.VMEM((3, 4, 4, 32, 8, 128), f32),
            pltpu.VMEM((3, 4, 4, 32, 8, 128), f32),
            pltpu.VMEM((4, 4, 32, 8, 128), f32),
            pltpu.VMEM((4, 4, 32, 8, 128), f32),
            pltpu.VMEM((4, 4, 32, 8, 128), f32),
            pltpu.VMEM(shape, jnp.int32),
            pltpu.VMEM(shape, jnp.int32),
            pltpu.VMEM((2,) + shape, f32),
            pltpu.VMEM((9, 8, 128), f32),
            pltpu.VMEM((2, 256, 256), jnp.bfloat16),
            pltpu.VMEM((256, 256), jnp.bfloat16),
            pltpu.VMEM((2, 8, 128), f32),
            pltpu.VMEM((3, 8, 128), f32),
            pltpu.VMEM((22, 8, 128), f32),
            dma((3, 3 * STEPS)),
            dma((3, 3 * STEPS)),
            dma((3, 3 * STEPS)),
            dma((3, 3 * STEPS)),
            dma((3 * STEPS,)),
            dma((3 * STEPS,)),
            dma((3,)),
            dma((3,)),
            dma((5,)),
            dma((2,)),
            dma((2,)),
        ],
        compiler_params=pltpu.CompilerParams(
            collective_id=0, has_side_effects=True, vmem_limit_bytes=58 << 20
        ),
        cost_estimate=pl.CostEstimate(flops=2 << 30, bytes_accessed=5 << 20, transcendentals=0),
    )(gamma_angle, beta_angle, *args)
    moved = pl.pallas_call(
        store_kernel,
        out_shape=(jax.ShapeDtypeStruct(shape, f32),) * 4,
        in_specs=[vmem] * 4,
        out_specs=(pl.BlockSpec(memory_space=pltpu.HBM),) * 4,
        scratch_shapes=[dma((4,))],
    )(*(pltpu.with_memory_space_constraint(v, pltpu.VMEM) for v in results[:4]))
    return tuple(v.reshape(-1) for v in moved) + (results[4], results[5])


def solution(mesh):
    whole = P(AXES)
    return jax.shard_map(
        per_device,
        mesh=mesh,
        in_specs=(whole,) * 5 + (P(), P()),
        out_specs=(whole,) * 4 + (P(), P()),
        check_vma=False,
    )
```

time: 93.8 us -> 70.3 us (0.75)
  Pallas kernels: 81.6 us -> 64.7 us
  local copies, waits for them, and re-layouts: 6.43 us -> 0 us
    pallas_call x1, Pallas kernels: 81.6 us -> 63.3 us  [per_device(): pl.pallas_call(kernel, out_shape=(big, big, big, big, one, one), in_specs...]
    unnamed x10 -> x0, local copies, waits for them, and re-layouts: 6.43 us -> none
    pallas_call x0 -> x1, Pallas kernels: none -> 1.35 us  [per_device(): pl.pallas_call(store_kernel, out_shape=(jax.ShapeDtypeStruct(shape, f32),...]
where the time goes in v2:
time: 70.3 us; the launch traced here: 70.2 us
  Pallas kernels  64.7 us (92%)
  between operations  5.46 us (8%)
    pallas_call x1, Pallas kernels, per_device(): pl.pallas_call(kernel, out_shape=(big, big, big, big, one, one), in_specs...  63.3 us

profile of v2, /device:TPU:1, one launch (start us, length us, event | category | flops | bytes accessed | tf_op | source)
XLA Modules:
  0.0 70.2 jit_solution(12582601479213335989)
XLA Ops:
  1.9 63.3 %shard_map.118 = (f32[4,32,8,128]{3,2,1,0:T(8,128)S(1)}, f32[4,32,8,128]{3,2,1,0:T(8,128)S(1)}, f32[4,32,8,128]{3,2,1,0:T(8,128)S(1)}, f32[4,32,8,128]{3,2,1,0:T(8,128)S(1)}, f32[1]{0:T(128)}, /*index=5*/f32[1]{0:T(128)}) custom-call(f32[1]{0:T(128)S(6)} %copy.15.gamma_ref, f32[1]{0:T(128)S(6)} %copy.16.beta_ref, f32[4,32,8,128]{3,2,1,0:T(8,128)} %bitcast.9, ...), custom_call_target="tpu_custom_call" | custom-call | flops 2147483648 | bytes 5242880 | tf_op jit(solution)/shard_map/pallas_call | solution.py:493
  65.3 1.3 %shard_map.119 = (f32[4,32,8,128]{3,2,1,0:T(8,128)}, f32[4,32,8,128]{3,2,1,0:T(8,128)}, f32[4,32,8,128]{3,2,1,0:T(8,128)}, f32[4,32,8,128]{3,2,1,0:T(8,128)}) custom-call(f32[4,32,8,128]{3,2,1,0:T(8,128)S(1)} %get-tuple-element.16.i0, f32[4,32,8,128]{3,2,1,0:T(8,128)S(1)} %get-tuple-element.17.i1, f32[4,32,8,128]{3,2,1,0:T(8,128)S(1)} %get-tuple-element.18.i2, ...), custom_call_target="tpu_custom_call" | custom-call | tf_op jit(solution)/shard_map/pallas_call | solution.py:530

commit v3 on v2

--- a/solution.py
+++ b/solution.py
@@ -11,12 +11,19 @@
 
 MESH = pl.DeviceIdType.MESH
 AXES = ("gx", "gy", "gz")
-STEPS = 3
-EARLY = 1
+STEPS = 4
+EARLY = 2
+
+
+def core_first(p, j):
+    return j % 2 == 1
+
+
+STORES = 4
 
 
 def cut(first, count):
-    sizes = [count // STEPS + (i < count % STEPS) for i in range(STEPS)]
+    sizes = [count // STEPS + (STEPS - 1 - i < count % STEPS) for i in range(STEPS)]
     return tuple((first + sum(sizes[:i]), sizes[i]) for i in range(STEPS))
 
 
@@ -111,11 +118,11 @@
     loads.append(pltpu.make_async_copy(energy_hbm, energy, in_sem.at[4]))
 
     barrier = pltpu.get_barrier_semaphore()
-    greeted = plane[1:] + group[1:]
+    greeted = [core_peer] + [peers[axis][k] for axis in range(3) for k in (1, 2, 3)]
+    for load in loads:
+        load.start()
     for device in greeted:
         pl.semaphore_signal(barrier, inc=1, device_id=device, device_id_type=MESH)
-    for load in loads:
-        load.start()
 
     def send(src, dst, send_sem, recv_sem, device):
         pltpu.make_async_remote_copy(
@@ -125,30 +132,32 @@
     def wait_bytes(ref, sem):
         pltpu.make_async_copy(ref, ref, sem).wait()
 
-    def start_there(f, p, j):
+    def source_of(f, p, j):
+        if f == 0:
+            return local_in
+        return home_b if core_first(p, j) == (f == 1) else home.at[f - 1]
+
+    def start_there(f, p, j, arrays=slice(None)):
         axis = (p + f) % 3
         r0, n = PARTS[p][j]
-        me, rows = place[axis], pl.ds(r0, n)
+        rows = pl.ds(r0, n)
         ss, rs = t_send.at[f, STEPS * p + j], t_recv.at[f, STEPS * p + j]
-        source = (local_in, home_b, home.at[1])[f]
+        source = source_of(f, p, j)
         for k in (2, 3, 1):
-            send(source.at[blocks[axis][k], :, rows], mid.at[f, me, :, rows], ss, rs, peers[axis][k])
-        pltpu.make_async_copy(source.at[me, :, rows], mid.at[f, me, :, rows], rs).start()
+            send(source.at[blocks[axis][k], arrays, rows], mid.at[f, k - 1, arrays, rows], ss, rs, peers[axis][k])
 
     def part_rows(p):
         return pl.ds(PARTS[p][0][0], sum(n for _, n in PARTS[p]))
 
     def start_energy(p):
         axis, rows = (p + 2) % 3, part_rows(p)
-        me = place[axis]
         for k in (2, 3, 1):
             block = blocks[axis][k]
-            send(energy_hbm.at[block, rows], energy_mid.at[me, rows], e_send.at[p], e_recv.at[p], peers[axis][k])
-        pltpu.make_async_copy(energy_hbm.at[me, rows], energy_mid.at[me, rows], e_recv.at[p]).start()
+            send(energy_hbm.at[block, rows], energy_mid.at[k - 1, rows], e_send.at[p], e_recv.at[p], peers[axis][k])
 
     def wait_energy(p):
         wait_bytes(energy_mid.at[:, part_rows(p)], e_recv.at[p])
-        wait_bytes(energy_mid.at[pl.ds(0, 3), part_rows(p)], e_send.at[p])
+        wait_bytes(energy_mid.at[:, part_rows(p)], e_send.at[p])
 
     def start_back(f, p, j):
         axis = (p + f) % 3
@@ -156,9 +165,7 @@
         me, rows = place[axis], pl.ds(r0, n)
         ss, rs = r_send.at[f, STEPS * p + j], r_recv.at[f, STEPS * p + j]
         for k in (2, 3, 1):
-            block = blocks[axis][k]
-            send(mid.at[f, block, :, rows], home.at[f, me, :, rows], ss, rs, peers[axis][k])
-        pltpu.make_async_copy(mid.at[f, me, :, rows], home.at[f, me, :, rows], rs).start()
+            send(mid.at[f, k - 1, :, rows], home.at[f, me, :, rows], ss, rs, peers[axis][k])
 
     def wait_there(f, p, j):
         rows = pl.ds(*PARTS[p][j])
@@ -166,12 +173,12 @@
 
     def wait_back(f, p, j):
         rows = pl.ds(*PARTS[p][j])
-        wait_bytes(home.at[f, :, :, rows], r_recv.at[f, STEPS * p + j])
+        wait_bytes(mid.at[f, :, :, rows], r_recv.at[f, STEPS * p + j])
 
     def wait_sent(f, p, j):
         rows = pl.ds(*PARTS[p][j])
-        wait_bytes(mid.at[f, pl.ds(0, 3), :, rows], t_send.at[f, STEPS * p + j])
-        wait_bytes(mid.at[f, pl.ds(0, 3), :, rows], r_send.at[f, STEPS * p + j])
+        wait_bytes(mid.at[f, :, :, rows], t_send.at[f, STEPS * p + j])
+        wait_bytes(mid.at[f, :, :, rows], r_send.at[f, STEPS * p + j])
 
     zero = jnp.zeros((8, 128), jnp.float32)
 
@@ -185,12 +192,16 @@
 
     def mix_axis(f, p, j):
         r0, n = PARTS[p][j]
+        me, source = place[(p + f) % 3], source_of(f, p, j)
         cc, ss, sc = (consts[i + (5 if f == 0 else 0)] for i in range(3))
         c, sn = consts[3], consts[4]
 
         def body(r, accs):
             acc, acc_gamma = accs
-            x = [[(mid[f, b, 2 * v, r], mid[f, b, 2 * v + 1, r]) for b in range(4)] for v in range(2)]
+            x = []
+            for v in range(2):
+                own = source[me, 2 * v, r], source[me, 2 * v + 1, r]
+                x.append([own] + [(mid[f, k, 2 * v, r], mid[f, k, 2 * v + 1, r]) for k in range(3)])
             s, s_outer, s_middle = mix_four(cc, ss, sc, x[0])
             a, a_outer, a_middle = mix_four(cc, ss, sc, x[1])
             acc = acc + inner(a_outer, s_middle) + inner(a_middle, s_outer)
@@ -203,11 +214,13 @@
                         s[b] = turn(c, sn, s[b], s_far)
                         a[b] = turn(c, sn, a[b], a_far)
                 if f == 2:
-                    acc_gamma = acc_gamma + energy_mid[b, r].astype(jnp.float32) * inner(a[b], s[b])
-                mid[f, b, 0, r] = s[b][0]
-                mid[f, b, 1, r] = s[b][1]
-                mid[f, b, 2, r] = a[b][0]
-                mid[f, b, 3, r] = a[b][1]
+                    level = energy_mid[b - 1, r] if b else energy[me, r]
+                    acc_gamma = acc_gamma + level.astype(jnp.float32) * inner(a[b], s[b])
+                for i, value in enumerate((*s[b], *a[b])):
+                    if b:
+                        mid[f, b - 1, i, r] = value
+                    else:
+                        home[f, me, i, r] = value
             return acc, acc_gamma
 
         acc, acc_gamma = lax.fori_loop(r0, r0 + n, body, (zero, zero))
@@ -215,7 +228,7 @@
         if f == 2:
             total[0] += acc_gamma
 
-    def mix_core_and_blocks(p, j):
+    def mix_core_and_blocks(f, p, j):
         r0, n = PARTS[p][j]
         cc, ss, sc, c, sn = (consts[i] for i in range(5))
 
@@ -224,7 +237,7 @@
             for v in range(2):
                 x.append([])
                 for b in range(4):
-                    own = home[0, b, 2 * v, r], home[0, b, 2 * v + 1, r]
+                    own = home[f, b, 2 * v, r], home[f, b, 2 * v + 1, r]
                     far = other[b, 2 * v, r], other[b, 2 * v + 1, r]
                     if v == 0:
                         x[v].append((own, far))
@@ -242,15 +255,15 @@
 
         total[1] += lax.fori_loop(r0, r0 + n, body, zero)
 
-    def mix_lanes(p, j):
+    def mix_lanes(f, p, j):
         r0, n = PARTS[p][j]
         rows, size = pl.ds(r0, n), n * 8
 
         def halves(v):
             parts = []
             for b in range(4):
-                re = home[1, b, 2 * v, rows].reshape(size, 128)
-                im = home[1, b, 2 * v + 1, rows].reshape(size, 128)
+                re = home[f, b, 2 * v, rows].reshape(size, 128)
+                im = home[f, b, 2 * v + 1, rows].reshape(size, 128)
                 parts.append(jnp.concatenate([re, im], axis=1))
             full = jnp.concatenate(parts, axis=0)
             high = full.astype(jnp.bfloat16)
@@ -266,8 +279,8 @@
         for v, (high, low) in enumerate(((s_high, s_low), (a_high, a_low))):
             mixed = dot(high, u_high) + (dot(low, u_high) + dot(high, u_low))
             for b in range(4):
-                home[1, b, 2 * v, rows] = mixed[b * size : (b + 1) * size, :128].reshape(n, 8, 128)
-                home[1, b, 2 * v + 1, rows] = mixed[b * size : (b + 1) * size, 128:].reshape(n, 8, 128)
+                home[f, b, 2 * v, rows] = mixed[b * size : (b + 1) * size, :128].reshape(n, 8, 128)
+                home[f, b, 2 * v + 1, rows] = mixed[b * size : (b + 1) * size, 128:].reshape(n, 8, 128)
 
     sn, c = sincos(jnp.full((8, 128), beta_ref[0], jnp.float32))
     scale_tiles = c * c * c * c * c
@@ -296,25 +309,26 @@
             local_in[b, 2 * v, r] = re
             local_in[b, 2 * v + 1, r] = im
 
-    def low_bits(i, carry):
-        for v in range(2):
-            mix_tiles(i // 4, v, [8 * (i % 4) + k for k in range(8)], 3)
+    def low_bits(v, i, carry):
+        mix_tiles(i // 4, v, [8 * (i % 4) + k for k in range(8)], 3)
         return carry
 
-    def high_bits(i, carry):
-        for v in range(2):
-            mix_tiles(i // 8, v, [i % 8 + 8 * k for k in range(4)], 2)
+    def high_bits(v, i, carry):
+        for half in range(2):
+            mix_tiles(i // 4, v, [2 * (i % 4) + half + 8 * k for k in range(4)], 2)
         return carry
 
     pl.semaphore_wait(barrier, len(greeted))
     for p in range(3):
         start_energy(p)
-    for load in loads[:4]:
-        load.wait()
-    lax.fori_loop(0, 16, low_bits, 0)
-    lax.fori_loop(0, 32, high_bits, 0)
-
-    for j in range(STEPS):
+    for v in range(2):
+        for load in loads[2 * v : 2 * v + 2]:
+            load.wait()
+        lax.fori_loop(0, 16, functools.partial(low_bits, v), 0)
+        lax.fori_loop(0, 16, functools.partial(high_bits, v), 0)
+        for p in range(3):
+            start_there(0, p, 0, pl.ds(2 * v, 2))
+    for j in range(1, STEPS):
         for p in range(3):
             start_there(0, p, j)
     loads[4].wait()
@@ -382,26 +396,31 @@
             mix_axis(0, p, j)
             start_back(0, p, j)
 
-    for j in range(STEPS):
-        for p in range(3):
-            rows = pl.ds(*PARTS[p][j])
-            wait_back(0, p, j)
-            send(home.at[0, :, :, rows], other.at[:, :, rows], c_send.at[STEPS * p + j], c_recv.at[STEPS * p + j], core_peer)
-        for p in range(3):
-            rows = pl.ds(*PARTS[p][j])
-            wait_bytes(other.at[:, :, rows], c_recv.at[STEPS * p + j])
-            mix_core_and_blocks(p, j)
-            start_there(1, p, j)
-    for j in range(STEPS):
-        for p in range(3):
-            wait_there(1, p, j)
-            mix_axis(1, p, j)
-            start_back(1, p, j)
-    for j in range(STEPS):
-        for p in range(3):
-            wait_back(1, p, j)
-            mix_lanes(p, j)
-            start_there(2, p, j)
+    def core_copy(f, p, j):
+        chunk, rows = STEPS * p + j, pl.ds(*PARTS[p][j])
+        return home.at[f, :, :, rows], other.at[:, :, rows], c_send.at[chunk], c_recv.at[chunk], core_peer
+
+    for f in range(2):
+        for j in range(STEPS):
+            with_core = [p for p in range(3) if core_first(p, j) == (f == 0)]
+            for p in range(3):
+                wait_back(f, p, j)
+                if p in with_core:
+                    send(*core_copy(f, p, j))
+            for p in range(3):
+                if p not in with_core:
+                    mix_lanes(f, p, j)
+                    start_there(f + 1, p, j)
+            for p in with_core:
+                wait_bytes(other.at[:, :, pl.ds(*PARTS[p][j])], c_recv.at[STEPS * p + j])
+                mix_core_and_blocks(f, p, j)
+                start_there(f + 1, p, j)
+        if f == 0:
+            for j in range(STEPS):
+                for p in range(3):
+                    wait_there(1, p, j)
+                    mix_axis(1, p, j)
+                    start_back(1, p, j)
     for p in range(3):
         wait_energy(p)
     for j in range(STEPS):
@@ -473,7 +492,11 @@
 
 
 def store_kernel(i0, i1, i2, i3, o0, o1, o2, o3, sem):
-    copies = [pltpu.make_async_copy(i, o, sem.at[k]) for k, (i, o) in enumerate(((i0, o0), (i1, o1), (i2, o2), (i3, o3)))]
+    copies = []
+    for k, (source, target) in enumerate(((i0, o0), (i1, o1), (i2, o2), (i3, o3))):
+        for b in range(STORES):
+            rows = pl.ds(b * (4 // STORES), 4 // STORES)
+            copies.append(pltpu.make_async_copy(source.at[rows], target.at[rows], sem.at[k, b]))
     for copy in copies:
         copy.start()
     for copy in copies:
@@ -496,13 +519,13 @@
         in_specs=[smem, smem] + [hbm] * 5,
         out_specs=(vmem, vmem, vmem, vmem, smem, smem),
         scratch_shapes=[
-            pltpu.VMEM((3, 4, 4, 32, 8, 128), f32),
+            pltpu.VMEM((3, 3, 4, 32, 8, 128), f32),
             pltpu.VMEM((3, 4, 4, 32, 8, 128), f32),
             pltpu.VMEM((4, 4, 32, 8, 128), f32),
             pltpu.VMEM((4, 4, 32, 8, 128), f32),
             pltpu.VMEM((4, 4, 32, 8, 128), f32),
             pltpu.VMEM(shape, jnp.int32),
-            pltpu.VMEM(shape, jnp.int32),
+            pltpu.VMEM((3, 32, 8, 128), jnp.int32),
             pltpu.VMEM((2,) + shape, f32),
             pltpu.VMEM((9, 8, 128), f32),
             pltpu.VMEM((2, 256, 256), jnp.bfloat16),
@@ -532,7 +555,7 @@
         out_shape=(jax.ShapeDtypeStruct(shape, f32),) * 4,
         in_specs=[vmem] * 4,
         out_specs=(pl.BlockSpec(memory_space=pltpu.HBM),) * 4,
-        scratch_shapes=[dma((4,))],
+        scratch_shapes=[dma((4, STORES))],
     )(*(pltpu.with_memory_space_constraint(v, pltpu.VMEM) for v in results[:4]))
     return tuple(v.reshape(-1) for v in moved) + (results[4], results[5])
 

time: 70.3 us -> 68.3 us (0.972)
  Pallas kernels: 64.7 us -> 62.7 us
    pallas_call x1, Pallas kernels: 63.3 us -> 61.2 us  [per_device(): pl.pallas_call(kernel, out_shape=(big, big, big, big, one, one), in_specs...]
where the time goes in v3:
time: 68.3 us; the launch traced here: 68.1 us
  Pallas kernels  62.7 us (92%)
  between operations  5.46 us (8%)
    pallas_call x1, Pallas kernels, per_device(): pl.pallas_call(kernel, out_shape=(big, big, big, big, one, one), in_specs...  61.2 us
    pallas_call x1, Pallas kernels, per_device(): pl.pallas_call(store_kernel, out_shape=(jax.ShapeDtypeStruct(shape, f32),...  1.44 us

profile of v3, /device:TPU:1, one launch (start us, length us, event | category | flops | bytes accessed | tf_op | source)
XLA Modules:
  0.0 68.1 jit_solution(2169338006249801297)
XLA Ops:
  1.9 61.2 %shard_map.118 = (f32[4,32,8,128]{3,2,1,0:T(8,128)S(1)}, f32[4,32,8,128]{3,2,1,0:T(8,128)S(1)}, f32[4,32,8,128]{3,2,1,0:T(8,128)S(1)}, f32[4,32,8,128]{3,2,1,0:T(8,128)S(1)}, f32[1]{0:T(128)}, /*index=5*/f32[1]{0:T(128)}) custom-call(f32[1]{0:T(128)S(6)} %copy.15.gamma_ref, f32[1]{0:T(128)S(6)} %copy.16.beta_ref, f32[4,32,8,128]{3,2,1,0:T(8,128)} %bitcast.9, ...), custom_call_target="tpu_custom_call" | custom-call | flops 2147483648 | bytes 5242880 | tf_op jit(solution)/shard_map/pallas_call | solution.py:516
  63.2 1.4 %shard_map.119 = (f32[4,32,8,128]{3,2,1,0:T(8,128)}, f32[4,32,8,128]{3,2,1,0:T(8,128)}, f32[4,32,8,128]{3,2,1,0:T(8,128)}, f32[4,32,8,128]{3,2,1,0:T(8,128)}) custom-call(f32[4,32,8,128]{3,2,1,0:T(8,128)S(1)} %get-tuple-element.16.i0, f32[4,32,8,128]{3,2,1,0:T(8,128)S(1)} %get-tuple-element.17.i1, f32[4,32,8,128]{3,2,1,0:T(8,128)S(1)} %get-tuple-element.18.i2, ...), custom_call_target="tpu_custom_call" | custom-call | tf_op jit(solution)/shard_map/pallas_call | solution.py:553

commit v4 on v3

--- a/solution.py
+++ b/solution.py
@@ -119,7 +119,7 @@
 
     barrier = pltpu.get_barrier_semaphore()
     greeted = [core_peer] + [peers[axis][k] for axis in range(3) for k in (1, 2, 3)]
-    for load in loads:
+    for load in loads[:4]:
         load.start()
     for device in greeted:
         pl.semaphore_signal(barrier, inc=1, device_id=device, device_id_type=MESH)
@@ -143,7 +143,7 @@
         rows = pl.ds(r0, n)
         ss, rs = t_send.at[f, STEPS * p + j], t_recv.at[f, STEPS * p + j]
         source = source_of(f, p, j)
-        for k in (2, 3, 1):
+        for k in (3, 1, 2):
             send(source.at[blocks[axis][k], arrays, rows], mid.at[f, k - 1, arrays, rows], ss, rs, peers[axis][k])
 
     def part_rows(p):
@@ -151,7 +151,7 @@
 
     def start_energy(p):
         axis, rows = (p + 2) % 3, part_rows(p)
-        for k in (2, 3, 1):
+        for k in (3, 1, 2):
             block = blocks[axis][k]
             send(energy_hbm.at[block, rows], energy_mid.at[k - 1, rows], e_send.at[p], e_recv.at[p], peers[axis][k])
 
@@ -164,7 +164,7 @@
         r0, n = PARTS[p][j]
         me, rows = place[axis], pl.ds(r0, n)
         ss, rs = r_send.at[f, STEPS * p + j], r_recv.at[f, STEPS * p + j]
-        for k in (2, 3, 1):
+        for k in (3, 1, 2):
             send(mid.at[f, k - 1, :, rows], home.at[f, me, :, rows], ss, rs, peers[axis][k])
 
     def wait_there(f, p, j):
@@ -331,7 +331,7 @@
     for j in range(1, STEPS):
         for p in range(3):
             start_there(0, p, j)
-    loads[4].wait()
+    loads[4].start()
 
     def build_lanes():
         c_row, s_row = (jnp.concatenate([consts[i], consts[i]], axis=0) for i in (3, 4))
@@ -388,6 +388,7 @@
         total[1] += lax.fori_loop(0, 128, body, zero) * consts[8]
 
     build_lanes()
+    loads[4].wait()
     build_trig()
     tile_bits_derivative()
     for j in range(STEPS):

time: 68.3 us -> 69.1 us (1.012)
  Pallas kernels: 62.7 us -> 63.5 us
    pallas_call x1, Pallas kernels: 61.2 us -> 62 us  [per_device(): pl.pallas_call(kernel, out_shape=(big, big, big, big, one, one), in_specs...]
where the time goes in v4:
time: 69.1 us; the launch traced here: 68.9 us
  Pallas kernels  63.5 us (92%)
  between operations  5.46 us (8%)
    pallas_call x1, Pallas kernels, per_device(): pl.pallas_call(kernel, out_shape=(big, big, big, big, one, one), in_specs...  62 us
    pallas_call x1, Pallas kernels, per_device(): pl.pallas_call(store_kernel, out_shape=(jax.ShapeDtypeStruct(shape, f32),...  1.44 us

profile of v4, /device:TPU:1, one launch (start us, length us, event | category | flops | bytes accessed | tf_op | source)
XLA Modules:
  0.0 68.9 jit_solution(9279879318122434901)
XLA Ops:
  1.9 62.0 %shard_map.118 = (f32[4,32,8,128]{3,2,1,0:T(8,128)S(1)}, f32[4,32,8,128]{3,2,1,0:T(8,128)S(1)}, f32[4,32,8,128]{3,2,1,0:T(8,128)S(1)}, f32[4,32,8,128]{3,2,1,0:T(8,128)S(1)}, f32[1]{0:T(128)}, /*index=5*/f32[1]{0:T(128)}) custom-call(f32[1]{0:T(128)S(6)} %copy.15.gamma_ref, f32[1]{0:T(128)S(6)} %copy.16.beta_ref, f32[4,32,8,128]{3,2,1,0:T(8,128)} %bitcast.9, ...), custom_call_target="tpu_custom_call" | custom-call | flops 2147483648 | bytes 5242880 | tf_op jit(solution)/shard_map/pallas_call | solution.py:517
  64.0 1.4 %shard_map.119 = (f32[4,32,8,128]{3,2,1,0:T(8,128)}, f32[4,32,8,128]{3,2,1,0:T(8,128)}, f32[4,32,8,128]{3,2,1,0:T(8,128)}, f32[4,32,8,128]{3,2,1,0:T(8,128)}) custom-call(f32[4,32,8,128]{3,2,1,0:T(8,128)S(1)} %get-tuple-element.16.i0, f32[4,32,8,128]{3,2,1,0:T(8,128)S(1)} %get-tuple-element.17.i1, f32[4,32,8,128]{3,2,1,0:T(8,128)S(1)} %get-tuple-element.18.i2, ...), custom_call_target="tpu_custom_call" | custom-call | tf_op jit(solution)/shard_map/pallas_call | solution.py:554
